TPU v7x, 512 devices: a whole 4x4x16 slice. The times are simulated.
512 devices in a mesh: blk: 8 (over y, core), uly: 16 (over z), tp: 4 (over x).
Axes of the slice: x: 4, y: 4, z: 16, core: 2. Of those that a mesh axis runs over, the one named last changes fastest.
Arguments:
- queries: bfloat16 [16384, 8192], P(('blk', 'uly'), 'tp'), parts along dimension 1, may hold values from -9 to 9
- keys: bfloat16 [16384, 1024], P(('blk', 'uly'), 'tp'), parts along dimension 1, may hold values from -9 to 9
- values: bfloat16 [16384, 1024], P(('blk', 'uly'), 'tp'), parts along dimension 1, may hold values from -6 to 6
- head_map: int32 [64], P('tp'), parts along dimension 0, may hold values from 0 to 1, as said below
- doc_lengths: int32 [32], replicated, may hold values from 1 to 2048, 16384 in all
- plan: int32 [8, 32], replicated, may hold values from 0 to 31, as said below
Outputs:
- output: bfloat16 [16384, 8192], P(('blk', 'uly'), 'tp'), parts along dimension 1
There are 4 independent parts, one for each index of `tp`. A program takes and returns all parts, laid end to end along the dimension named above; an argument that names none is the same for every part. Nothing has to cross between parts.
Inputs may be any that keep to these rules, and one draw needn't show every extreme that they name: `head_map`: each key-value head serves exactly 8 query heads. Each row plan[s] is a permutation of 0 to 31.
All inputs are finite; a program needn't handle non-finite values.
Results may differ from a plain program's by a relative error of at most 0.0036.
Values may be sent and summed in bfloat16 or wider, within the bound.
A program may use at most 64 MiB of HBM per device.

v0:
```python
import math

import jax
import jax.numpy as jnp
from jax import lax
from jax.sharding import PartitionSpec as P

DH = 128


NEG_START = -1e30


def sent_together(arrays, axis, split_dim, concat_dim, along):
    ends, at = ([], 0)
    for a in arrays[:-1]:
        at += a.shape[along]
        ends.append(at)
    both = jnp.concatenate(arrays, axis=along)
    return tuple(
        jnp.split(
            lax.all_to_all(both, axis, split_axis=split_dim, concat_axis=concat_dim, tiled=True),
            ends,
            axis=along,
        )
    )


def passed_along(x, axis, by):
    count = lax.axis_size(axis)
    pairs = [(i, i + by) for i in range(count) if 0 <= i + by < count]
    return lax.ppermute(x, axis, pairs)


def segment_of(positions, doc_ends):
    return jnp.sum((positions[:, None] >= doc_ends[None, :]).astype(jnp.int32), axis=1)


def attend(running, query_tile, query_pos, key_tile, value_tile, key_pos, doc_ends):
    row_max, row_total, summed = running
    scale = 1.0 / math.sqrt(query_tile.shape[-1])
    scores = (
        jnp.einsum("rhd,shd->rhs", query_tile, key_tile, preferred_element_type=jnp.float32) * scale
    )
    same_doc = segment_of(query_pos, doc_ends)[:, None] == segment_of(key_pos, doc_ends)[None, :]
    visible = same_doc & (key_pos[None, :] <= query_pos[:, None]) & (key_pos[None, :] >= 0)
    scores = jnp.where(visible[:, None, :], scores, -jnp.inf)
    new_max = jnp.maximum(row_max, jnp.max(scores, axis=-1))
    weights = jnp.exp(scores - new_max[..., None])
    rescale = jnp.exp(row_max - new_max)
    row_total = row_total * rescale + jnp.sum(weights, axis=-1)
    summed = summed * rescale[..., None] + jnp.einsum(
        "rhs,shd->rhd", weights.astype(jnp.bfloat16), value_tile, preferred_element_type=jnp.float32
    )
    return (new_max, row_total, summed)


def body(queries, keys, values, head_map, doc_lengths, plan):
    tokens = queries.shape[0]
    heads = head_map.shape[0]
    width = DH
    kv_heads = keys.shape[1] // width
    uly_count = lax.axis_size("uly")
    blk_count = lax.axis_size("blk")
    local_heads = heads // uly_count
    stretch = tokens * uly_count
    pieces = plan.shape[1]
    block = stretch // pieces
    group = stretch // blk_count
    blk_index = lax.axis_index("blk")
    doc_ends = jnp.cumsum(doc_lengths)
    query_rows = queries.reshape(tokens, heads, width)
    key_rows = keys.reshape(tokens, kv_heads, width)
    value_rows = values.reshape(tokens, kv_heads, width)
    chooser = (head_map[:, None] == jnp.arange(kv_heads, dtype=jnp.int32)[None, :]).astype(
        jnp.bfloat16
    )
    key_wide = jnp.einsum(
        "tkd,hk->thd", key_rows, chooser, preferred_element_type=jnp.float32
    ).astype(jnp.bfloat16)
    value_wide = jnp.einsum(
        "tkd,hk->thd", value_rows, chooser, preferred_element_type=jnp.float32
    ).astype(jnp.bfloat16)
    query_stretch, key_stretch, value_stretch = sent_together(
        (query_rows, key_wide, value_wide), "uly", 1, 0, 2
    )
    plan_row = lax.dynamic_index_in_dim(plan, blk_index, 0, keepdims=False)
    prior_key, prior_value = passed_along((key_stretch, value_stretch), "blk", 1)
    key_pair = jnp.concatenate([prior_key, key_stretch], axis=0)
    value_pair = jnp.concatenate([prior_value, value_stretch], axis=0)
    key_first = (blk_index - 1) * stretch
    tile = math.gcd(512, stretch)
    tiles = stretch // tile
    doc_starts = doc_ends - doc_lengths
    doc_numbers = jnp.arange(doc_lengths.shape[0], dtype=jnp.int32)

    def one_tile(tile_index):
        row_start = tile_index * tile
        query_tile = lax.dynamic_slice_in_dim(query_stretch, row_start, tile, 0)
        query_pos = blk_index * stretch + row_start + jnp.arange(tile, dtype=jnp.int32)
        first_doc = segment_of(query_pos[:1], doc_ends)
        first_start = jnp.sum(jnp.where(doc_numbers == first_doc, doc_starts, 0))
        lowest = jnp.maximum((first_start - key_first) // tile, 0)

        def key_step(step, running):
            key_tile = lax.dynamic_slice_in_dim(key_pair, step * tile, tile, 0)
            value_tile = lax.dynamic_slice_in_dim(value_pair, step * tile, tile, 0)
            key_pos = key_first + step * tile + jnp.arange(tile, dtype=jnp.int32)
            return attend(running, query_tile, query_pos, key_tile, value_tile, key_pos, doc_ends)

        start_state = (
            jnp.full((tile, local_heads), NEG_START, jnp.float32),
            jnp.zeros((tile, local_heads), jnp.float32),
            jnp.zeros((tile, local_heads, width), jnp.float32),
        )
        row_max, row_total, summed = lax.fori_loop(
            lowest, tiles + tile_index + 1, key_step, start_state
        )
        return (summed / row_total[..., None]).astype(jnp.bfloat16)

    attended = lax.map(one_tile, jnp.arange(tiles, dtype=jnp.int32)).reshape(
        stretch, local_heads, width
    )
    sending = attended.reshape(pieces, block, local_heads, width)[plan_row].reshape(
        blk_count, group, local_heads, width
    )
    stored = lax.all_to_all(sending, "blk", split_axis=0, concat_axis=0, tiled=True).reshape(
        stretch, local_heads, width
    )
    returned = lax.all_to_all(stored, "uly", split_axis=0, concat_axis=1, tiled=True)
    return returned.reshape(tokens, heads * width)


def solution(mesh):
    return jax.shard_map(
        body,
        mesh=mesh,
        in_specs=(
            P(("blk", "uly"), "tp"),
            P(("blk", "uly"), "tp"),
            P(("blk", "uly"), "tp"),
            P("tp"),
            P(),
            P(),
        ),
        out_specs=P(("blk", "uly"), "tp"),
        check_vma=False,
    )
```

profile of v0, /device:TPU:4, one launch (start us, length us, event | category | flops | bytes accessed | tf_op | source)
XLA Modules:
  0.0 208.5 jit_solution(13464266036653270253)
XLA Ops:
  0.0 0.9 reshape.236
  0.9 0.9 reshape.237
  1.8 1.0 fusion.22
  2.8 1.0 fusion.23
  4.0 0.2 pad_maximum_fusion
  4.2 0.4 copy.24
  4.6 89.0 %all_to_all.38 = bf16[128,16,384]{2,0,1:T(8,128)(2,1)S(1)} all-to-all(bf16[128,16,384]{2,0,1:T(8,128)(2,1)S(1)} %copy.24), channel_id=1, replica_groups=mesh['blk'=8,'uly'=16,'tp'=4] {'uly'}, dimensions={1} | all-to-all | bytes 3145728 | tf_op jit(solution)/shard_map/all_to_all | solution.py:22
  93.6 0.3 fusion.30
  93.9 1.3 collective-permute-start.1
  95.3 0.7 fusion.26
  96.0 5.0 %collective-permute-start = (bf16[2048,1,128]{2,0,1:T(8,128)(2,1)S(1)}, bf16[2048,1,128]{2,0,1:T(8,128)(2,1)}, u32[]{:S(2)}, u32[]{:S(2)}) collective-permute-start(bf16[2048,1,128]{2,0,1:T(8,128)(2,1)S(1)} %get-tuple-element.319), channel_id=1, source_target_pairs={{0,64},{64,128},{128,192},{192,256},{256,320},{320,384},{384,448},... | collective-permute-start | bytes 1572872 | tf_op jit(solution)/shard_map/ppermute | solution.py:32
  101.3 0.5 collective-permute-done
  101.8 1.1 pad_maximum_fusion.1
  102.9 34.3 %while.42 = (s32[]{:T(128)}, bf16[4,512,1,128]{3,1,0,2:T(8,128)(2,1)}, s32[4]{0:T(128)S(1)}, s32[]{:T(128)}, s32[32]{0:T(128)S(1)}, /*index=5*/s32[32]{0:T(128)S...) while((s32[]{:T(128)}, ...), condition=%wide.region_10.11_spmd.clone, body=%wide.region_1.10_spmd.clone.sunk | while | flops 137464528 | bytes 5569236 | solution.py:121
  102.9 0.6 dynamic_slice.45
  104.1 0.5 slice.10
  104.6 1.3 fusion.41
  105.9 1.3 fusion.42
  108.5 1.2 while.43
  108.6 0.5 fusion.46
  109.1 0.2 fusion.47
  109.3 0.4 fusion.48
  109.9 0.7 constant_dynamic-update-slice_fusion.2
  110.6 0.6 dynamic_slice.45
  111.7 0.5 slice.10
  112.3 1.3 fusion.41
  113.6 1.3 fusion.42
  116.1 2.5 %while.43 = (s32[]{:T(128)}, f32[512,1]{0,1:T(1,128)S(1)}, f32[512,1]{0,1:T(1,128)S(1)}, f32[512,1,128]{0,2,1:T(8,128)S(1)}, s32[]{:T(128)}, /*index=5*/s32[32]{...) while((s32[]{:T(128)}, f32[512,1]{0,1:T(1,128)S(1)}, ...), condition=%wide.region_9.9_spmd.clone, body=%wide.region_4.8_spmd.clone.sunk | while | flops 137332736 | bytes 4117851 | solution.py:116
  116.3 0.5 fusion.46
  116.8 0.2 fusion.47
  117.0 0.4 fusion.48
  117.5 0.5 fusion.46
  118.2 0.4 fusion.48
  118.8 0.7 constant_dynamic-update-slice_fusion.2
  119.5 0.6 dynamic_slice.45
  120.6 0.5 slice.10
  121.2 1.3 fusion.41
  122.5 1.3 fusion.42
  125.0 2.5 %while.43 = (s32[]{:T(128)}, f32[512,1]{0,1:T(1,128)S(1)}, f32[512,1]{0,1:T(1,128)S(1)}, f32[512,1,128]{0,2,1:T(8,128)S(1)}, s32[]{:T(128)}, /*index=5*/s32[32]{...) while((s32[]{:T(128)}, f32[512,1]{0,1:T(1,128)S(1)}, ...), condition=%wide.region_9.9_spmd.clone, body=%wide.region_4.8_spmd.clone.sunk | while | flops 137332736 | bytes 4117851 | solution.py:116
  125.2 0.5 fusion.46
  125.9 0.4 fusion.48
  126.4 0.5 fusion.46
  127.1 0.4 fusion.48
  127.7 0.7 constant_dynamic-update-slice_fusion.2
  128.4 0.6 dynamic_slice.45
  129.5 0.5 slice.10
  130.1 1.3 fusion.41
  131.4 1.3 fusion.42
  133.9 2.5 %while.43 = (s32[]{:T(128)}, f32[512,1]{0,1:T(1,128)S(1)}, f32[512,1]{0,1:T(1,128)S(1)}, f32[512,1,128]{0,2,1:T(8,128)S(1)}, s32[]{:T(128)}, /*index=5*/s32[32]{...) while((s32[]{:T(128)}, f32[512,1]{0,1:T(1,128)S(1)}, ...), condition=%wide.region_9.9_spmd.clone, body=%wide.region_4.8_spmd.clone.sunk | while | flops 137332736 | bytes 4117851 | solution.py:116
  134.1 0.5 fusion.46
  134.6 0.2 fusion.47
  134.8 0.4 fusion.48
  135.3 0.5 fusion.46
  135.8 0.2 fusion.47
  136.0 0.4 fusion.48
  136.6 0.7 constant_dynamic-update-slice_fusion.2
  137.2 1.7 gather_fusion
  138.9 31.5 %all_to_all.39 = bf16[8,256,1,128]{3,1,2,0:T(8,128)(2,1)S(1)} all-to-all(bf16[8,256,1,128]{3,1,2,0:T(8,128)(2,1)S(1)} %bitcast.106), channel_id=1, replica_groups=mesh['blk'=8,'uly'=16,'tp'=4] {'blk'}, dimensions={0} | all-to-all | bytes 1048576 | tf_op jit(solution)/shard_map/all_to_all | solution.py:127
  170.5 0.5 broadcast.162
  171.0 1.0 reduce.7
  172.1 34.5 %all_to_all.40 = bf16[16,2,8192]{2,1,0:T(2,128)(2,1)S(1)} all-to-all(bf16[16,2,8192]{2,1,0:T(2,128)(2,1)S(1)} %reshape.259), channel_id=1, replica_groups=mesh['blk'=8,'uly'=16,'tp'=4] {'uly'}, dimensions={0} | all-to-all | bytes 1048576 | tf_op jit(solution)/shard_map/all_to_all | solution.py:130
  206.6 0.5 reshape.260
  207.2 0.3 copy.28
  207.5 1.0 copy.29
  (89 shorter events, 2.9 us)
Async XLA Ops:
  0.0 3.9 %copy-start = (bf16[128,2048]{1,0:T(8,128)(2,1)S(1)}, bf16[128,2048]{1,0:T(8,128)(2,1)}, u32[]{:S(2)}) copy-start(bf16[128,2048]{1,0:T(8,128)(2,1)} %param.10) | copy-start | bytes 1572868
  93.6 7.3 %copy-start.1 = (s32[32]{0:T(128)S(1)}, s32[32]{0:T(128)}, u32[]{:S(2)}) copy-start(s32[32]{0:T(128)} %param.14) | copy-start | bytes 388
  93.9 7.3 %collective-permute-start.1 = (bf16[2048,1,128]{2,0,1:T(8,128)(2,1)S(1)}, bf16[2048,1,128]{2,0,1:T(8,128)(2,1)S(1)}, u32[]{:S(2)}, u32[]{:S(2)}) collective-permute-start(bf16[2048,1,128]{2,0,1:T(8,128)(2,1)S(1)} %get-tuple-element.318), channel_id=1, source_target_pairs={{0,64},{64,128},{128,192},{192,256},{256,320},{320,384},{384,448},... | collective-permute-start | bytes 1572872 | tf_op jit(solution)/shard_map/ppermute | solution.py:32
  96.0 5.8 %collective-permute-start = (bf16[2048,1,128]{2,0,1:T(8,128)(2,1)S(1)}, bf16[2048,1,128]{2,0,1:T(8,128)(2,1)}, u32[]{:S(2)}, u32[]{:S(2)}) collective-permute-start(bf16[2048,1,128]{2,0,1:T(8,128)(2,1)S(1)} %get-tuple-element.319), channel_id=1, source_target_pairs={{0,64},{64,128},{128,192},{192,256},{256,320},{320,384},{384,448},... | collective-permute-start | bytes 1572872 | tf_op jit(solution)/shard_map/ppermute | solution.py:32
where the time goes:
time: 208 us; the launch traced here: 209 us
  blocking collectives  155 us (75%)
  other arithmetic  16.1 us (8%)
  local copies, waits for them, and re-layouts  14.6 us (7%)
  matrix products  7.95 us (4%)
  loops' own time  7.89 us (4%)
  starting transfers between devices  6.28 us (3%)
    all_to_all x1, blocking collectives, sent_together(): lax.all_to_all(both, axis, split_axis=split_dim, concat_axis=concat_dim,...  89 us
    all_to_all x1, blocking collectives, body(): lax.all_to_all(stored, 'uly', split_axis=0, concat_axis=1, tiled=True)  34.5 us
    all_to_all x1, blocking collectives, body(): lax.all_to_all(sending, 'blk', split_axis=0, concat_axis=0, tiled=True)  31.5 us
    another operation x1, loops' own time, body(): lax.map(one_tile, jnp.arange(tiles, dtype=jnp.int32))  7.35 us
    ppermute x2, starting transfers between devices, passed_along(): return lax.ppermute(x, axis, pairs)  6.28 us
    reduce_sum x11, other arithmetic, segment_of(): jnp.sum((positions[:, None] >= doc_ends[None, :]).astype(jnp.int32), axis=1)  5.88 us
    reduce_sum x4, other arithmetic, one_tile(): first_start = jnp.sum(jnp.where(doc_numbers == first_doc, doc_starts, 0))  5.16 us
  transfers between devices with their start and end apart: 2, of which 1 were waited for; matrix products, arithmetic and copies ran while one was open for 0% of the time, Pallas kernels for 0%

commit v1 on v0

v1 whole, which is shorter than its diff:
```python
import functools
import math

import jax
import jax.numpy as jnp
from jax import lax
from jax.experimental import pallas as pl
from jax.experimental.pallas import tpu as pltpu
from jax.sharding import PartitionSpec as P

DH = 128
MESH = pl.DeviceIdType.MESH
VMEM = pltpu.VMEM
SMEM = pltpu.SMEM
NEG = -1e30


def slot_of(head_map, h, heads, kv_heads):
    per = heads // kv_heads
    mine = head_map[h]
    before = jnp.int32(0)
    for g in range(h):
        before += (head_map[g] == mine).astype(jnp.int32)
    return mine * per + before


def spread_kernel(nb, nz, hm, q, k, v, qo, kvo, sq, skv, rq, rkv, sems):
    b, u = lax.axis_index("blk"), lax.axis_index("uly")
    heads = hm.shape[0]
    tokens = q.shape[0]
    kvh = k.shape[1] // DH
    part = tokens // nb
    (s1q_s, s1q_r, s1k_s, s1k_r, s2q_s, s2q_r, s2c_s, s2c_r, s2p_s, s2p_r, gy_s, gy_r, gc_s, gc_r) = sems

    barrier = pltpu.get_barrier_semaphore()
    for d in range(1, nb):
        pl.semaphore_signal(barrier, inc=1, device_id={"blk": lax.rem(b + d, nb)}, device_id_type=MESH)
    for d in range(1, nz):
        pl.semaphore_signal(barrier, inc=1, device_id={"uly": lax.rem(u + d, nz)}, device_id_type=MESH)

    slots = [slot_of(hm, h, heads, kvh) for h in range(heads)]

    def head_at(i):
        at = jnp.int32(0)
        for h in range(heads):
            at += h * (slots[h] == i).astype(jnp.int32)
        return at

    for i in range(nb):
        for e in range(kvh):
            skv[i, e, 0] = k[i * part : (i + 1) * part, e * DH : (e + 1) * DH]
            skv[i, e, 1] = v[i * part : (i + 1) * part, e * DH : (e + 1) * DH]

    pl.semaphore_wait(barrier, nb - 1 + nz - 1)

    s1k, s1q = [], []
    for d in list(range(1, nb)) + [0]:
        to = lax.rem(b + d, nb)
        if d == 0:
            c = pltpu.make_async_copy(skv.at[to], rkv.at[b], s1k_r.at[b])
        else:
            c = pltpu.make_async_remote_copy(
                src_ref=skv.at[to], dst_ref=rkv.at[b], send_sem=s1k_s.at[d], recv_sem=s1k_r.at[b],
                device_id={"blk": to}, device_id_type=MESH)
        c.start()
        s1k.append((d, c))
    for d in list(range(1, nb)) + [0]:
        to = lax.rem(b + d, nb)
        for e in range(kvh):
            sq[to, e] = q[:, pl.ds(head_at(e * nb + to) * DH, DH)]
        if d == 0:
            c = pltpu.make_async_copy(sq.at[to], rq.at[b], s1q_r.at[b])
        else:
            c = pltpu.make_async_remote_copy(
                src_ref=sq.at[to], dst_ref=rq.at[b], send_sem=s1q_s.at[d], recv_sem=s1q_r.at[b],
                device_id={"blk": to}, device_id_type=MESH)
        c.start()
        s1q.append((d, c))

    def arrived(dst, sem):
        pltpu.make_async_copy(dst, dst, sem).wait()

    for s in range(nb):
        arrived(rkv.at[s], s1k_r.at[s])

    zorder = [0]
    for d in range(1, nz // 2 + 1):
        zorder += [d] if d == nz - d else [d, nz - d]
    zorder = zorder[1:][::-1] + [0]
    sent = []
    for d in zorder:
        to = lax.rem(u + d, nz)
        s, e = to // kvh, lax.rem(to, kvh)
        prior = lax.rem(s + nb - 1, nb)
        for cp, src_s, ss, rs in ((1, s, s2c_s, s2c_r), (0, prior, s2p_s, s2p_r)):
            src, dst = rkv.at[src_s, e], kvo.at[:, cp * nz + u, b]
            if d == 0:
                c = pltpu.make_async_copy(src, dst, rs.at[u])
            else:
                c = pltpu.make_async_remote_copy(
                    src_ref=src, dst_ref=dst, send_sem=ss.at[d], recv_sem=rs.at[u],
                    device_id={"uly": to}, device_id_type=MESH)
            c.start()
            sent.append((d, c))
    for s in range(nb):
        arrived(rq.at[s], s1q_r.at[s])
    for d in zorder:
        to = lax.rem(u + d, nz)
        s, e = to // kvh, lax.rem(to, kvh)
        if d == 0:
            c = pltpu.make_async_copy(rq.at[s, e], qo.at[u], s2q_r.at[u])
        else:
            c = pltpu.make_async_remote_copy(
                src_ref=rq.at[s, e], dst_ref=qo.at[u], send_sem=s2q_s.at[d], recv_sem=s2q_r.at[u],
                device_id={"uly": to}, device_id_type=MESH)
        c.start()
        sent.append((d, c))

    for z in range(nz):
        arrived(kvo.at[:, nz + z, b], s2c_r.at[z])
        arrived(kvo.at[:, z, b], s2p_r.at[z])

    other = b + 1 - 2 * lax.rem(b, 2)
    mine = kvo.at[:, :, b]
    for d in range(1, nb // 2):
        c = pltpu.make_async_remote_copy(
            src_ref=mine, dst_ref=mine, send_sem=gy_s.at[d], recv_sem=gy_r.at[d],
            device_id={"blk": lax.rem(b + 2 * d, nb)}, device_id_type=MESH)
        c.start()
        sent.append((1, c))
    for d in range(nb // 2):
        at = lax.rem(b + nb - 2 * d, nb)
        block = kvo.at[:, :, at]
        if d > 0:
            arrived(block, gy_r.at[d])
        c = pltpu.make_async_remote_copy(
            src_ref=block, dst_ref=block, send_sem=gc_s.at[d], recv_sem=gc_r.at[d],
            device_id={"blk": other}, device_id_type=MESH)
        c.start()
        sent.append((1, c))
    for d in range(nb // 2):
        arrived(kvo.at[:, :, lax.rem(other + nb - 2 * d, nb)], gc_r.at[d])
    for z in range(nz):
        arrived(qo.at[z], s2q_r.at[z])
    for d, c in s1k + s1q + sent:
        if d != 0:
            c.wait_send()


def attend_kernel(nz, kvh, tile, chunk, lengths, q, k, v, o, lo_t):
    stretch = q.shape[0]
    s = lax.axis_index("uly") // kvh
    base = (s - 1) * stretch
    lanes = lo_t.shape[0]
    rows = stretch // lanes
    pos = lax.broadcasted_iota(jnp.int32, (lanes, lanes), 0) * lanes + lax.broadcasted_iota(
        jnp.int32, (lanes, lanes), 1) + s * stretch
    first = jnp.zeros((lanes, lanes), jnp.int32)
    start = jnp.int32(0)
    for n in range(lengths.shape[0]):
        first = jnp.where(pos >= start, start, first)
        start = start + lengths[n]
    lo_t[...] = jnp.transpose((first - base).astype(jnp.float32))
    scale = math.log2(math.e) / math.sqrt(DH)
    ones = jnp.ones((chunk, DH), jnp.bfloat16)

    def one_tile(t, _):
        row0 = t * tile
        qt = q[pl.ds(row0, tile), :]
        lane = lax.broadcasted_iota(jnp.int32, (lanes, lanes), 1)
        cols = [
            jnp.sum(jnp.where(lane == t * (tile // lanes) + i, lo_t[...], 0.0), axis=1, keepdims=True)
            for i in range(tile // lanes)
        ]
        lo = jnp.concatenate(cols, axis=0).astype(jnp.int32)
        p0 = s * stretch + row0
        begin = jnp.int32(0)
        at = jnp.int32(0)
        for n in range(lengths.shape[0]):
            begin = jnp.where(p0 >= at, at, begin)
            at = at + lengths[n]
        lowest = (begin - base) // chunk
        last = (stretch + row0 + tile + chunk - 1) // chunk
        hi = stretch + row0 + lax.broadcasted_iota(jnp.int32, (tile, 1), 0)

        def key_step(c, carry):
            m, acc = carry
            kt = k[pl.ds(c * chunk, chunk), :]
            vt = v[pl.ds(c * chunk, chunk), :]
            sc = lax.dot_general(qt, kt, (((1,), (1,)), ((), ())), preferred_element_type=jnp.float32)
            key = c * chunk + lax.broadcasted_iota(jnp.int32, (tile, chunk), 1)
            sc = jnp.where((key >= lo) & (key <= hi), sc, NEG)
            new_m = jnp.maximum(m, jnp.max(sc, axis=1, keepdims=True))
            p = jnp.where(sc <= NEG, 0.0, jnp.exp2((sc - new_m) * scale))
            alpha = jnp.exp2((m - new_m) * scale)
            both = jnp.concatenate([vt, ones], axis=1)
            acc = acc * alpha + jnp.dot(p.astype(jnp.bfloat16), both, preferred_element_type=jnp.float32)
            return new_m, acc

        m, acc = lax.fori_loop(
            lowest, last, key_step,
            (jnp.full((tile, 1), NEG, jnp.float32), jnp.zeros((tile, 2 * DH), jnp.float32)))
        o[pl.ds(row0, tile), :] = (acc[:, :DH] / acc[:, DH:]).astype(jnp.bfloat16)
        return 0

    lax.fori_loop(0, stretch // tile, one_tile, 0)


def return_kernel(nb, nz, kvh, hm, plan, a, o, sa, ra, ss, rs):
    b, u = lax.axis_index("blk"), lax.axis_index("uly")
    s, e = u // kvh, lax.rem(u, kvh)
    heads = hm.shape[0]
    pieces = a.shape[0]
    per = pieces // (nb * kvh)
    barrier = pltpu.get_barrier_semaphore()
    peers = [(d, f) for f in range(kvh) for d in range(nb) if (d, f) != (0, 0)]

    def where(d, f):
        return {"blk": lax.rem(b + d, nb), "uly": s * kvh + lax.rem(e + f, kvh)}

    for d, f in peers:
        pl.semaphore_signal(barrier, inc=1, device_id=where(d, f), device_id_type=MESH)
    for i in range(pieces):
        sa[i] = a[plan[s, i]]
    pl.semaphore_wait(barrier, len(peers))
    slot = e * nb + b
    copies = []
    for d, f in peers + [(0, 0)]:
        to = where(d, f)
        src = sa.at[pl.ds((to["blk"] * kvh + to["uly"] - s * kvh) * per, per)]
        if (d, f) == (0, 0):
            pltpu.make_async_copy(src, ra.at[slot], rs.at[slot]).start()
        else:
            c = pltpu.make_async_remote_copy(
                src_ref=src, dst_ref=ra.at[slot], send_sem=ss.at[d * kvh + f], recv_sem=rs.at[slot],
                device_id=to, device_id_type=MESH)
            c.start()
            copies.append(c)
    for i in range(heads):
        pltpu.make_async_copy(ra.at[i], ra.at[i], rs.at[i]).wait()
    for h in range(heads):
        o[:, h * DH : (h + 1) * DH] = ra[slot_of(hm, h, heads, kvh)].reshape(o.shape[0], DH)
    for c in copies:
        c.wait_send()


def body(queries, keys, values, head_map, doc_lengths, plan):
    nb, nz = lax.axis_size("blk"), lax.axis_size("uly")
    tokens = queries.shape[0]
    kvh = keys.shape[1] // DH
    stretch = tokens * nz
    part = tokens // nb
    heads = head_map.shape[0]
    pieces = plan.shape[1]
    block = stretch // pieces
    bf = jnp.bfloat16
    dma = pltpu.SemaphoreType.DMA
    vm = pl.BlockSpec(memory_space=VMEM)
    sm = pl.BlockSpec(memory_space=SMEM)

    qs, kvs = pl.pallas_call(
        functools.partial(spread_kernel, nb, nz),
        out_shape=(
            jax.ShapeDtypeStruct((nz, tokens, DH), bf),
            jax.ShapeDtypeStruct((2, 2 * nz, nb, part, DH), bf),
        ),
        in_specs=[sm, vm, vm, vm],
        out_specs=(vm, vm),
        scratch_shapes=[
            VMEM((nb, kvh, tokens, DH), bf),
            VMEM((nb, kvh, 2, part, DH), bf),
            VMEM((nb, kvh, tokens, DH), bf),
            VMEM((nb, kvh, 2, part, DH), bf),
            [dma((n,)) for n in (nb, nb, nb, nb, nz, nz, nz, nz, nz, nz, nb // 2, nb // 2, nb // 2, nb // 2)],
        ],
        compiler_params=pltpu.CompilerParams(collective_id=0, has_side_effects=True, vmem_limit_bytes=40 << 20),
        name="spread",
    )(head_map, queries, keys, values)

    attended = pl.pallas_call(
        functools.partial(attend_kernel, nz, kvh, 256, 512),
        out_shape=jax.ShapeDtypeStruct((stretch, DH), bf),
        in_specs=[sm, vm, vm, vm],
        out_specs=vm,
        scratch_shapes=[VMEM((128, 128), jnp.float32)],
        compiler_params=pltpu.CompilerParams(vmem_limit_bytes=40 << 20),
        name="attend",
    )(doc_lengths, qs.reshape(stretch, DH), kvs[0].reshape(2 * stretch, DH), kvs[1].reshape(2 * stretch, DH))

    return pl.pallas_call(
        functools.partial(return_kernel, nb, nz, kvh),
        out_shape=jax.ShapeDtypeStruct((tokens, heads * DH), bf),
        in_specs=[sm, sm, vm],
        out_specs=vm,
        scratch_shapes=[
            VMEM((pieces, block, DH), bf),
            VMEM((heads, tokens // block, block, DH), bf),
            dma((heads,)),
            dma((heads,)),
        ],
        compiler_params=pltpu.CompilerParams(collective_id=1, has_side_effects=True, vmem_limit_bytes=40 << 20),
        name="give_back",
    )(head_map, plan, attended.reshape(pieces, block, DH))


def solution(mesh):
    return jax.shard_map(
        body,
        mesh=mesh,
        in_specs=(
            P(("blk", "uly"), "tp"),
            P(("blk", "uly"), "tp"),
            P(("blk", "uly"), "tp"),
            P("tp"),
            P(),
            P(),
        ),
        out_specs=P(("blk", "uly"), "tp"),
        check_vma=False,
    )
```

time: 208 us -> 94.4 us (0.45)
  the two profiles are of different devices: /device:TPU:4 before, /device:TPU:65 now
where the time goes in v1:
time: 94.4 us; the launch traced here: 94.1 us
  Pallas kernels  89.2 us (94%)
  local copies, waits for them, and re-layouts  4.84 us (5%)
    pallas_call x1, Pallas kernels, body(): pl.pallas_call(functools.partial(spread_kernel, nb, nz), out_shape=(jax.S...  56.3 us
    pallas_call x1, Pallas kernels, body(): pl.pallas_call(functools.partial(attend_kernel, nz, kvh, 256, 512), out_s...  20.2 us
    pallas_call x1, Pallas kernels, body(): pl.pallas_call(functools.partial(return_kernel, nb, nz, kvh), out_shape=j...  12.7 us
    unnamed x13, local copies, waits for them, and re-layouts  4.18 us

profile of v1, /device:TPU:65, one launch (start us, length us, event | category | flops | bytes accessed | tf_op | source)
XLA Modules:
  0.0 94.1 jit_solution(6063525498849015957)
XLA Ops:
  0.0 0.0 copy-start
  0.0 1.0 %copy-done = bf16[128,2048]{1,0:T(8,128)(2,1)S(1)} copy-done((bf16[128,2048]{1,0:T(8,128)(2,1)S(1)}, bf16[128,2048]{1,0:T(8,128)(2,1)}, u32[]{:S(2)}) %copy-start) | copy-done | bytes 524312
  1.0 0.0 copy-start.1
  1.0 0.8 copy-done.1
  1.9 0.0 copy-start.2
  1.9 0.8 copy-done.2
  2.7 0.0 copy-start.4
  2.7 0.7 copy-done.4
  3.4 56.3 %spread.1 = (bf16[16,128,128]{2,1,0:T(8,128)(2,1)S(1)}, bf16[2,32,8,16,128]{4,3,2,1,0:T(8,128)(2,1)S(1)}) custom-call(s32[16]{0:T(128)S(1)} %copy-done.4, bf16[128,2048]{1,0:T(8,128)(2,1)S(1)} %copy-done, bf16[128,256]{1,0:T(8,128)(2,1)S(1)} %copy-done.1, bf16[128,256]{1,0:T(8,128)(2,1)S(1)} %copy-done.2), custom_call_target="tpu_custom_call" | custom-call | tf_op jit(solution)/shard_map/spread/pallas_call | solution.py:261
  59.7 0.0 copy-start.5
  59.7 0.7 fusion
  60.4 0.0 copy-start.3
  60.4 0.0 copy-done.5
  60.4 20.2 %attend.1 = bf16[2048,128]{1,0:T(8,128)(2,1)S(1)} custom-call(s32[32]{0:T(128)S(1)} %copy-done.5, bf16[2048,128]{1,0:T(8,128)(2,1)S(1)} %bitcast.7, bf16[4096,128]{1,0:T(8,128)(2,1)S(1)} %bitcast.5, bf16[4096,128]{1,0:T(8,128)(2,1)S(1)} %bitcast.4), custom_call_target="tpu_custom_call" | custom-call | tf_op jit(solution)/shard_map/attend/pallas_call | solution.py:280
  80.6 0.0 copy-done.3
  80.6 12.7 %give_back.1 = bf16[128,2048]{1,0:T(8,128)(2,1)S(1)} custom-call(s32[16]{0:T(128)S(1)} %copy-done.4, s32[8,32]{1,0:T(8,128)S(1)} %copy-done.3, bf16[32,64,128]{2,1,0:T(8,128)(2,1)S(1)} %bitcast.6), custom_call_target="tpu_custom_call" | custom-call | tf_op jit(solution)/shard_map/give_back/pallas_call | solution.py:290
  93.3 0.8 copy.8
Async XLA Ops:
  0.0 1.0 %copy-start = (bf16[128,2048]{1,0:T(8,128)(2,1)S(1)}, bf16[128,2048]{1,0:T(8,128)(2,1)}, u32[]{:S(2)}) copy-start(bf16[128,2048]{1,0:T(8,128)(2,1)} %q.1) | copy-start | bytes 1572868
  1.0 0.8 copy-start.1
  1.9 0.8 copy-start.2
  2.7 0.7 copy-start.4
  59.7 0.7 copy-start.5
  60.4 20.2 %copy-start.3 = (s32[8,32]{1,0:T(8,128)S(1)}, s32[8,32]{1,0:T(8,128)}, u32[]{:S(2)}) copy-start(s32[8,32]{1,0:T(8,128)} %plan.1) | copy-start | bytes 3076

commit v2 on v0

v2 whole, which is shorter than its diff:
```python
import functools
import math

import jax
import jax.numpy as jnp
from jax import lax
from jax.experimental import pallas as pl
from jax.experimental.pallas import tpu as pltpu
from jax.sharding import PartitionSpec as P

DH = 128
MESH = pl.DeviceIdType.MESH
VMEM = pltpu.VMEM
SMEM = pltpu.SMEM
NEG = -1e30


def slot_of(head_map, h, heads, kv_heads):
    per = heads // kv_heads
    mine = head_map[h]
    before = jnp.int32(0)
    for g in range(h):
        before += (head_map[g] == mine).astype(jnp.int32)
    return mine * per + before


def fused_kernel(nb, nz, hm, lengths, plan, q_hbm, k_hbm, v_hbm, o, q, sq, skv, rq, rkv, qo, kvo, att, sa, ra, lo_t, sc, sems):
    b, u = lax.axis_index("blk"), lax.axis_index("uly")
    heads = hm.shape[0]
    tokens = q.shape[0]
    kvh = skv.shape[1]
    pieces = att.shape[0]
    per = pieces // (nb * kvh)
    stretch = tokens * nz
    window = nz + 1
    (s1q_s, s1q_r, s1k_s, s1k_r, s2q_s, s2q_r, s2c_s, s2c_r, s2p_s, s2p_r, gy_s, gy_r, gc_s, gc_r, rt_s, rt_r, in_s) = sems
    my_s, my_e = u // kvh, lax.rem(u, kvh)

    def remote(src, dst, ss, rs, **to):
        return pltpu.make_async_remote_copy(
            src_ref=src, dst_ref=dst, send_sem=ss, recv_sem=rs, device_id=to, device_id_type=MESH)

    def arrived(dst, sem):
        pltpu.make_async_copy(dst, dst, sem).wait()

    loads = []
    for e in range(kvh):
        for i, ref in enumerate((k_hbm, v_hbm)):
            c = pltpu.make_async_copy(ref.at[:, :, e * DH : (e + 1) * DH], skv.at[:, e, i], in_s.at[2 * e + i])
            c.start()
            loads.append(c)
    load_q = pltpu.make_async_copy(q_hbm, q, in_s.at[2 * kvh])
    load_q.start()

    barrier = pltpu.get_barrier_semaphore()
    twin = [(d, f) for f in range(1, kvh) for d in range(1, nb)]
    for d in range(1, nb):
        pl.semaphore_signal(barrier, inc=1, device_id={"blk": lax.rem(b + d, nb)}, device_id_type=MESH)
    for d in range(1, nz):
        pl.semaphore_signal(barrier, inc=1, device_id={"uly": lax.rem(u + d, nz)}, device_id_type=MESH)
    for d, f in twin:
        pl.semaphore_signal(
            barrier, inc=1, device_id={"blk": lax.rem(b + d, nb), "uly": my_s * kvh + lax.rem(my_e + f, kvh)},
            device_id_type=MESH)
    for c in loads:
        c.wait()
    pl.semaphore_wait(barrier, nb - 1 + nz - 1 + len(twin))

    sent = []
    near = []
    for d in range(1, nb // 2 + 1):
        near += [d] if d == nb - d else [d, nb - d]
    for d in near + [0]:
        to = lax.rem(b + d, nb)
        if d == 0:
            pltpu.make_async_copy(skv.at[to], rkv.at[b], s1k_r.at[b]).start()
        else:
            c = remote(skv.at[to], rkv.at[b], s1k_s.at[d], s1k_r.at[b], blk=to)
            c.start()
            sent.append(c)
    slots = [slot_of(hm, h, heads, kvh) for h in range(heads)]

    def head_at(i):
        at = jnp.int32(0)
        for h in range(heads):
            at += h * (slots[h] == i).astype(jnp.int32)
        return at

    load_q.wait()
    for d in near + [0]:
        to = lax.rem(b + d, nb)
        for e in range(kvh):
            sq[to, e] = q[:, pl.ds(head_at(e * nb + to) * DH, DH)]
        if d == 0:
            pltpu.make_async_copy(sq.at[to], rq.at[b], s1q_r.at[b]).start()
        else:
            c = remote(sq.at[to], rq.at[b], s1q_s.at[d], s1q_r.at[b], blk=to)
            c.start()
            sent.append(c)
    for s in range(nb):
        arrived(rkv.at[s], s1k_r.at[s])

    znear = []
    for d in range(1, nz // 2 + 1):
        znear += [d] if d == nz - d else [d, nz - d]
    for cp, ss, rs in ((1, s2c_s, s2c_r), (0, s2p_s, s2p_r)):
        for d in znear + [0]:
            to = lax.rem(u + d, nz)
            s, e = to // kvh, lax.rem(to, kvh)
            src = rkv.at[s if cp else lax.rem(s + nb - 1, nb), e]
            dst = kvo.at[:, cp * nz + u, b]
            if d == 0:
                pltpu.make_async_copy(src, dst, rs.at[u]).start()
            else:
                c = remote(src, dst, ss.at[d], rs.at[u], uly=to)
                c.start()
                sent.append(c)
    for s in range(nb):
        arrived(rq.at[s], s1q_r.at[s])
    for d in znear + [0]:
        to = lax.rem(u + d, nz)
        s, e = to // kvh, lax.rem(to, kvh)
        if d == 0:
            pltpu.make_async_copy(rq.at[s, e], qo.at[u], s2q_r.at[u]).start()
        else:
            c = remote(rq.at[s, e], qo.at[u], s2q_s.at[d], s2q_r.at[u], uly=to)
            c.start()
            sent.append(c)

    row = lax.broadcasted_iota(jnp.int32, (tokens, tokens), 0)
    pos = row * tokens + lax.broadcasted_iota(jnp.int32, (tokens, tokens), 1) + my_s * stretch
    first = jnp.zeros((tokens, tokens), jnp.int32)
    start = jnp.int32(0)
    for n in range(lengths.shape[0]):
        first = jnp.where(pos >= start, start, first)
        start = start + lengths[n]
    lo_t[...] = jnp.transpose((first - (my_s - 1) * stretch - row * tokens).astype(jnp.float32))

    other = b + 1 - 2 * lax.rem(b, 2)
    half = nb // 2
    for cp, rs in ((1, s2c_r), (0, s2p_r)):
        for z in range(nz):
            arrived(kvo.at[:, cp * nz + z, b], rs.at[z])
        mine = kvo.at[:, cp * nz : (cp + 1) * nz, b]
        for d in range(1, half):
            c = remote(mine, mine, gy_s.at[cp * half + d], gy_r.at[cp * half + d], blk=lax.rem(b + 2 * d, nb))
            c.start()
            sent.append(c)
        c = remote(mine, mine, gc_s.at[cp * half], gc_r.at[cp * half], blk=other)
        c.start()
        sent.append(c)
    for cp in (1, 0):
        for d in range(1, half):
            block = kvo.at[:, cp * nz : (cp + 1) * nz, lax.rem(b + nb - 2 * d, nb)]
            arrived(block, gy_r.at[cp * half + d])
            c = remote(block, block, gc_s.at[cp * half + d], gc_r.at[cp * half + d], blk=other)
            c.start()
            sent.append(c)
    for cp in (1, 0):
        for d in range(half):
            arrived(kvo.at[:, cp * nz : (cp + 1) * nz, lax.rem(other + nb - 2 * d, nb)], gc_r.at[cp * half + d])

    scale = math.log2(math.e) / math.sqrt(DH)
    chunks = [(c, min(2, window - c)) for c in range(0, window, 2)]

    def one_tile(i, _):
        d = jnp.where(lax.rem(i, 2) == 1, (i + 1) // 2, nz - i // 2)
        z = lax.rem(u + d, nz)
        arrived(qo.at[z], s2q_r.at[z])
        qt = qo[z]
        lane = lax.broadcasted_iota(jnp.int32, (tokens, tokens), 1)
        lo = jnp.sum(jnp.where(lane == z, lo_t[...], 0.0), axis=1, keepdims=True).astype(jnp.int32)
        lo = jnp.broadcast_to(lo, (tokens, tokens))
        causal = lane <= lax.broadcasted_iota(jnp.int32, (tokens, tokens), 0)
        top = jnp.full((tokens, tokens), NEG, jnp.float32)
        for c, n in chunks:
            kt = kvo[0, pl.ds(z + c, n)].reshape(n * tokens, DH)
            s = lax.dot_general(qt, kt, (((1,), (1,)), ((), ())), preferred_element_type=jnp.float32)
            for j in range(n):
                seen = lane >= lo - (c + j) * tokens
                if c + j == window - 1:
                    seen = seen & causal
                sj = jnp.where(seen, s[:, j * tokens : (j + 1) * tokens], NEG)
                sc[:, (c + j) * tokens : (c + j + 1) * tokens] = sj
                top = jnp.maximum(top, sj)
        m = jnp.max(top, axis=1, keepdims=True)
        acc = jnp.zeros((tokens, 2 * DH), jnp.float32)
        for c, n in chunks:
            p = jnp.exp2((sc[:, c * tokens : (c + n) * tokens] - m) * scale).astype(jnp.bfloat16)
            vt = kvo[1, pl.ds(z + c, n)].reshape(n * tokens, DH)
            both = jnp.concatenate([vt, jnp.ones_like(vt)], axis=1)
            acc = acc + jnp.dot(p, both, preferred_element_type=jnp.float32)
        out = (acc[:, :DH] / acc[:, DH:]).astype(jnp.bfloat16)
        att[pl.ds(z * (tokens // att.shape[1]), tokens // att.shape[1])] = out.reshape(tokens // att.shape[1], att.shape[1], DH)
        return 0

    lax.fori_loop(0, nz, one_tile, 0)

    for i in range(pieces):
        sa[i] = att[plan[my_s, i]]
    slot = my_e * nb + b
    for d, f in [(d, f) for f in range(kvh) for d in near] + [(0, f) for f in range(kvh - 1, -1, -1)]:
        tb, te = lax.rem(b + d, nb), lax.rem(my_e + f, kvh)
        src = sa.at[pl.ds((tb * kvh + te) * per, per)]
        if (d, f) == (0, 0):
            pltpu.make_async_copy(src, ra.at[slot], rt_r.at[slot]).start()
        else:
            c = remote(src, ra.at[slot], rt_s.at[d * kvh + f], rt_r.at[slot], blk=tb, uly=my_s * kvh + te)
            c.start()
            sent.append(c)
    for i in range(heads):
        arrived(ra.at[i], rt_r.at[i])
    for h in range(heads):
        o[:, h * DH : (h + 1) * DH] = ra[slot_of(hm, h, heads, kvh)].reshape(tokens, DH)
    for c in sent:
        c.wait_send()


def body(queries, keys, values, head_map, doc_lengths, plan):
    nb, nz = lax.axis_size("blk"), lax.axis_size("uly")
    tokens = queries.shape[0]
    kvh = keys.shape[1] // DH
    stretch = tokens * nz
    part = tokens // nb
    heads = head_map.shape[0]
    pieces = plan.shape[1]
    block = stretch // pieces
    bf = jnp.bfloat16
    dma = pltpu.SemaphoreType.DMA
    sm = pl.BlockSpec(memory_space=SMEM)
    hbm = pl.BlockSpec(memory_space=pl.ANY)
    return pl.pallas_call(
        functools.partial(fused_kernel, nb, nz),
        out_shape=jax.ShapeDtypeStruct((tokens, heads * DH), bf),
        in_specs=[sm, sm, sm, hbm, hbm, hbm],
        out_specs=pl.BlockSpec(memory_space=VMEM),
        scratch_shapes=[
            VMEM((tokens, heads * DH), bf),
            VMEM((nb, kvh, tokens, DH), bf),
            VMEM((nb, kvh, 2, part, DH), bf),
            VMEM((nb, kvh, tokens, DH), bf),
            VMEM((nb, kvh, 2, part, DH), bf),
            VMEM((nz, tokens, DH), bf),
            VMEM((2, 2 * nz, nb, part, DH), bf),
            VMEM((pieces, block, DH), bf),
            VMEM((pieces, block, DH), bf),
            VMEM((heads, tokens // block, block, DH), bf),
            VMEM((tokens, tokens), jnp.float32),
            VMEM((tokens, (nz + 1) * tokens), jnp.float32),
            [dma((n,)) for n in (nb, nb, nb, nb, nz, nz, nz, nz, nz, nz, nb, nb, nb, nb, heads, heads, 2 * kvh + 1)],
        ],
        compiler_params=pltpu.CompilerParams(collective_id=0, has_side_effects=True, vmem_limit_bytes=63 << 20),
        name="fused",
    )(head_map, doc_lengths, plan, queries, keys.reshape(nb, part, kvh * DH), values.reshape(nb, part, kvh * DH))


def solution(mesh):
    return jax.shard_map(
        body,
        mesh=mesh,
        in_specs=(
            P(("blk", "uly"), "tp"),
            P(("blk", "uly"), "tp"),
            P(("blk", "uly"), "tp"),
            P("tp"),
            P(),
            P(),
        ),
        out_specs=P(("blk", "uly"), "tp"),
        check_vma=False,
    )
```

time: 208 us -> 75.6 us (0.36)
  the two profiles are of different devices: /device:TPU:4 before, /device:TPU:1 now
where the time goes in v2:
time: 75.6 us; the launch traced here: 75.4 us
  Pallas kernels  73.5 us (97%)
  local copies, waits for them, and re-layouts  1.88 us (2%)
    pallas_call x1, Pallas kernels, body(): pl.pallas_call(functools.partial(fused_kernel, nb, nz), out_shape=jax.Sha...  73.5 us
    unnamed x1, local copies, waits for them, and re-layouts  1.88 us

profile of v2, /device:TPU:1, one launch (start us, length us, event | category | flops | bytes accessed | tf_op | source)
XLA Modules:
  0.0 75.4 jit_solution(13492175011656174087)
XLA Ops:
  0.0 73.5 %fused.1 = bf16[128,2048]{1,0:T(8,128)(2,1)} custom-call(s32[16]{0:T(128)} %hm.1, s32[32]{0:T(128)} %lengths.1, s32[8,32]{1,0:T(8,128)} %plan.1, bf16[128,2048]{1,0:T(8,128)(2,1)} %q_hbm.1, bf16[8,16,256]{2,1,0:T(8,128)(2,1)} %bitcast.2, bf16[8,16,256]{2,1,0:T(8,128)(2,1)} %bitcast.3), custom_call_target="tpu_custom_call" | custom-call | tf_op jit(solution)/shard_map/fused/pallas_call | solution.py:232
  73.5 1.9 %copy.8 = bf16[128,2048]{1,0:T(8,128)(2,1)} copy(bf16[128,2048]{1,0:T(8,128)(2,1)} %fused.1) | data formatting | bytes 1048576

commit v3 on v2

--- a/solution.py
+++ b/solution.py
@@ -43,15 +43,6 @@
     def arrived(dst, sem):
         pltpu.make_async_copy(dst, dst, sem).wait()
 
-    loads = []
-    for e in range(kvh):
-        for i, ref in enumerate((k_hbm, v_hbm)):
-            c = pltpu.make_async_copy(ref.at[:, :, e * DH : (e + 1) * DH], skv.at[:, e, i], in_s.at[2 * e + i])
-            c.start()
-            loads.append(c)
-    load_q = pltpu.make_async_copy(q_hbm, q, in_s.at[2 * kvh])
-    load_q.start()
-
     barrier = pltpu.get_barrier_semaphore()
     twin = [(d, f) for f in range(1, kvh) for d in range(1, nb)]
     for d in range(1, nb):
@@ -62,22 +53,15 @@
         pl.semaphore_signal(
             barrier, inc=1, device_id={"blk": lax.rem(b + d, nb), "uly": my_s * kvh + lax.rem(my_e + f, kvh)},
             device_id_type=MESH)
-    for c in loads:
-        c.wait()
-    pl.semaphore_wait(barrier, nb - 1 + nz - 1 + len(twin))
-
-    sent = []
-    near = []
-    for d in range(1, nb // 2 + 1):
-        near += [d] if d == nb - d else [d, nb - d]
-    for d in near + [0]:
-        to = lax.rem(b + d, nb)
-        if d == 0:
-            pltpu.make_async_copy(skv.at[to], rkv.at[b], s1k_r.at[b]).start()
-        else:
-            c = remote(skv.at[to], rkv.at[b], s1k_s.at[d], s1k_r.at[b], blk=to)
-            c.start()
-            sent.append(c)
+    loads = []
+    for e in range(kvh):
+        for i, ref in enumerate((k_hbm, v_hbm)):
+            c = pltpu.make_async_copy(ref.at[:, :, e * DH : (e + 1) * DH], skv.at[:, e, i], in_s.at[2 * e + i])
+            c.start()
+            loads.append(c)
+    load_q = pltpu.make_async_copy(q_hbm, q, in_s.at[2 * kvh])
+    load_q.start()
+
     slots = [slot_of(hm, h, heads, kvh) for h in range(heads)]
 
     def head_at(i):
@@ -86,17 +70,33 @@
             at += h * (slots[h] == i).astype(jnp.int32)
         return at
 
-    load_q.wait()
-    for d in near + [0]:
-        to = lax.rem(b + d, nb)
+    def pack(to):
         for e in range(kvh):
             sq[to, e] = q[:, pl.ds(head_at(e * nb + to) * DH, DH)]
-        if d == 0:
-            pltpu.make_async_copy(sq.at[to], rq.at[b], s1q_r.at[b]).start()
-        else:
-            c = remote(sq.at[to], rq.at[b], s1q_s.at[d], s1q_r.at[b], blk=to)
-            c.start()
-            sent.append(c)
+
+    near = []
+    for d in range(1, nb // 2 + 1):
+        near += [d] if d == nb - d else [d, nb - d]
+    for c in loads:
+        c.wait()
+    load_q.wait()
+    for d in [0] + near:
+        pack(lax.rem(b + d, nb))
+    pl.semaphore_wait(barrier, nb - 1 + nz - 1 + len(twin))
+
+    sent = []
+    for d in near:
+        to = lax.rem(b + d, nb)
+        c = remote(skv.at[to], rkv.at[b], s1k_s.at[d], s1k_r.at[b], blk=to)
+        c.start()
+        sent.append(c)
+    pltpu.make_async_copy(skv.at[b], rkv.at[b], s1k_r.at[b]).start()
+    for d in near:
+        to = lax.rem(b + d, nb)
+        c = remote(sq.at[to], rq.at[b], s1q_s.at[d], s1q_r.at[b], blk=to)
+        c.start()
+        sent.append(c)
+    pltpu.make_async_copy(sq.at[b], rq.at[b], s1q_r.at[b]).start()
     for s in range(nb):
         arrived(rkv.at[s], s1k_r.at[s])
 
@@ -117,15 +117,12 @@
                 sent.append(c)
     for s in range(nb):
         arrived(rq.at[s], s1q_r.at[s])
-    for d in znear + [0]:
+    pltpu.make_async_copy(rq.at[my_s, my_e], qo.at[u], s2q_r.at[u]).start()
+    for d in znear:
         to = lax.rem(u + d, nz)
-        s, e = to // kvh, lax.rem(to, kvh)
-        if d == 0:
-            pltpu.make_async_copy(rq.at[s, e], qo.at[u], s2q_r.at[u]).start()
-        else:
-            c = remote(rq.at[s, e], qo.at[u], s2q_s.at[d], s2q_r.at[u], uly=to)
-            c.start()
-            sent.append(c)
+        c = remote(rq.at[to // kvh, lax.rem(to, kvh)], qo.at[u], s2q_s.at[d], s2q_r.at[u], uly=to)
+        c.start()
+        sent.append(c)
 
     row = lax.broadcasted_iota(jnp.int32, (tokens, tokens), 0)
     pos = row * tokens + lax.broadcasted_iota(jnp.int32, (tokens, tokens), 1) + my_s * stretch
@@ -163,10 +160,7 @@
     scale = math.log2(math.e) / math.sqrt(DH)
     chunks = [(c, min(2, window - c)) for c in range(0, window, 2)]
 
-    def one_tile(i, _):
-        d = jnp.where(lax.rem(i, 2) == 1, (i + 1) // 2, nz - i // 2)
-        z = lax.rem(u + d, nz)
-        arrived(qo.at[z], s2q_r.at[z])
+    def one_tile(z, sc):
         qt = qo[z]
         lane = lax.broadcasted_iota(jnp.int32, (tokens, tokens), 1)
         lo = jnp.sum(jnp.where(lane == z, lo_t[...], 0.0), axis=1, keepdims=True).astype(jnp.int32)
@@ -192,14 +186,22 @@
             acc = acc + jnp.dot(p, both, preferred_element_type=jnp.float32)
         out = (acc[:, :DH] / acc[:, DH:]).astype(jnp.bfloat16)
         att[pl.ds(z * (tokens // att.shape[1]), tokens // att.shape[1])] = out.reshape(tokens // att.shape[1], att.shape[1], DH)
+
+    def two_tiles(i, _):
+        near_z = lax.rem(u + i + 1, nz)
+        far_z = lax.rem(u + jnp.where(i == nz // 2 - 1, 0, nz - 1 - i), nz)
+        for z in (near_z, far_z):
+            arrived(qo.at[z], s2q_r.at[z])
+        one_tile(near_z, sc.at[0])
+        one_tile(far_z, sc.at[1])
         return 0
 
-    lax.fori_loop(0, nz, one_tile, 0)
+    lax.fori_loop(0, nz // 2, two_tiles, 0)
 
     for i in range(pieces):
         sa[i] = att[plan[my_s, i]]
     slot = my_e * nb + b
-    for d, f in [(d, f) for f in range(kvh) for d in near] + [(0, f) for f in range(kvh - 1, -1, -1)]:
+    for d, f in [(d, f) for f in range(kvh - 1, -1, -1) for d in near[::-1]] + [(0, f) for f in range(kvh - 1, -1, -1)]:
         tb, te = lax.rem(b + d, nb), lax.rem(my_e + f, kvh)
         src = sa.at[pl.ds((tb * kvh + te) * per, per)]
         if (d, f) == (0, 0):
@@ -246,7 +248,7 @@
             VMEM((pieces, block, DH), bf),
             VMEM((heads, tokens // block, block, DH), bf),
             VMEM((tokens, tokens), jnp.float32),
-            VMEM((tokens, (nz + 1) * tokens), jnp.float32),
+            VMEM((2, tokens, (nz + 1) * tokens), jnp.float32),
             [dma((n,)) for n in (nb, nb, nb, nb, nz, nz, nz, nz, nz, nz, nb, nb, nb, nb, heads, heads, 2 * kvh + 1)],
         ],
         compiler_params=pltpu.CompilerParams(collective_id=0, has_side_effects=True, vmem_limit_bytes=63 << 20),

time: 75.6 us -> 73.4 us (0.971)
  Pallas kernels: 73.5 us -> 71.3 us
    pallas_call x1, Pallas kernels: 73.5 us -> 71.3 us  [body(): pl.pallas_call(functools.partial(fused_kernel, nb, nz), out_shape=jax.Sha...]
where the time goes in v3:
time: 73.4 us; the launch traced here: 73.2 us
  Pallas kernels  71.3 us (97%)
  local copies, waits for them, and re-layouts  1.88 us (3%)
    pallas_call x1, Pallas kernels, body(): pl.pallas_call(functools.partial(fused_kernel, nb, nz), out_shape=jax.Sha...  71.3 us
    unnamed x1, local copies, waits for them, and re-layouts  1.88 us

profile of v3, /device:TPU:1, one launch (start us, length us, event | category | flops | bytes accessed | tf_op | source)
XLA Modules:
  0.0 73.2 jit_solution(12463003281925424545)
XLA Ops:
  0.0 71.3 %fused.1 = bf16[128,2048]{1,0:T(8,128)(2,1)} custom-call(s32[16]{0:T(128)} %hm.1, s32[32]{0:T(128)} %lengths.1, s32[8,32]{1,0:T(8,128)} %plan.1, bf16[128,2048]{1,0:T(8,128)(2,1)} %q_hbm.1, bf16[8,16,256]{2,1,0:T(8,128)(2,1)} %bitcast.2, bf16[8,16,256]{2,1,0:T(8,128)(2,1)} %bitcast.3), custom_call_target="tpu_custom_call" | custom-call | tf_op jit(solution)/shard_map/fused/pallas_call | solution.py:234
  71.3 1.9 %copy.8 = bf16[128,2048]{1,0:T(8,128)(2,1)} copy(bf16[128,2048]{1,0:T(8,128)(2,1)} %fused.1) | data formatting | bytes 1048576

commit v4 on v3

--- a/solution.py
+++ b/solution.py
@@ -24,7 +24,7 @@
     return mine * per + before
 
 
-def fused_kernel(nb, nz, hm, lengths, plan, q_hbm, k_hbm, v_hbm, o, q, sq, skv, rq, rkv, qo, kvo, att, sa, ra, lo_t, sc, sems):
+def fused_kernel(nb, nz, hm_hbm, lengths_hbm, plan_hbm, q_hbm, k_hbm, v_hbm, o, q, sq, skv, rq, rkv, qo, kvo, att, sa, lo_t, sc, hm, lengths, plan, sems):
     b, u = lax.axis_index("blk"), lax.axis_index("uly")
     heads = hm.shape[0]
     tokens = q.shape[0]
@@ -54,6 +54,10 @@
             barrier, inc=1, device_id={"blk": lax.rem(b + d, nb), "uly": my_s * kvh + lax.rem(my_e + f, kvh)},
             device_id_type=MESH)
     loads = []
+    for i, (ref, to) in enumerate(((hm_hbm, hm), (lengths_hbm, lengths), (plan_hbm, plan))):
+        c = pltpu.make_async_copy(ref, to, in_s.at[2 * kvh + 1 + i])
+        c.start()
+        loads.append(c)
     for e in range(kvh):
         for i, ref in enumerate((k_hbm, v_hbm)):
             c = pltpu.make_async_copy(ref.at[:, :, e * DH : (e + 1) * DH], skv.at[:, e, i], in_s.at[2 * e + i])
@@ -62,6 +66,8 @@
     load_q = pltpu.make_async_copy(q_hbm, q, in_s.at[2 * kvh])
     load_q.start()
 
+    for c in loads:
+        c.wait()
     slots = [slot_of(hm, h, heads, kvh) for h in range(heads)]
 
     def head_at(i):
@@ -77,8 +83,6 @@
     near = []
     for d in range(1, nb // 2 + 1):
         near += [d] if d == nb - d else [d, nb - d]
-    for c in loads:
-        c.wait()
     load_q.wait()
     for d in [0] + near:
         pack(lax.rem(b + d, nb))
@@ -104,7 +108,7 @@
     for d in range(1, nz // 2 + 1):
         znear += [d] if d == nz - d else [d, nz - d]
     for cp, ss, rs in ((1, s2c_s, s2c_r), (0, s2p_s, s2p_r)):
-        for d in znear + [0]:
+        for d in znear[::-1] + [0]:
             to = lax.rem(u + d, nz)
             s, e = to // kvh, lax.rem(to, kvh)
             src = rkv.at[s if cp else lax.rem(s + nb - 1, nb), e]
@@ -118,7 +122,7 @@
     for s in range(nb):
         arrived(rq.at[s], s1q_r.at[s])
     pltpu.make_async_copy(rq.at[my_s, my_e], qo.at[u], s2q_r.at[u]).start()
-    for d in znear:
+    for d in znear[::-1]:
         to = lax.rem(u + d, nz)
         c = remote(rq.at[to // kvh, lax.rem(to, kvh)], qo.at[u], s2q_s.at[d], s2q_r.at[u], uly=to)
         c.start()
@@ -188,8 +192,8 @@
         att[pl.ds(z * (tokens // att.shape[1]), tokens // att.shape[1])] = out.reshape(tokens // att.shape[1], att.shape[1], DH)
 
     def two_tiles(i, _):
-        near_z = lax.rem(u + i + 1, nz)
-        far_z = lax.rem(u + jnp.where(i == nz // 2 - 1, 0, nz - 1 - i), nz)
+        near_z = lax.rem(u + nz // 2 - i, nz)
+        far_z = lax.rem(u + jnp.where(i == 0, 0, nz // 2 + i), nz)
         for z in (near_z, far_z):
             arrived(qo.at[z], s2q_r.at[z])
         one_tile(near_z, sc.at[0])
@@ -205,17 +209,21 @@
         tb, te = lax.rem(b + d, nb), lax.rem(my_e + f, kvh)
         src = sa.at[pl.ds((tb * kvh + te) * per, per)]
         if (d, f) == (0, 0):
-            pltpu.make_async_copy(src, ra.at[slot], rt_r.at[slot]).start()
+            pltpu.make_async_copy(src, o.at[slot], rt_r.at[slot]).start()
         else:
-            c = remote(src, ra.at[slot], rt_s.at[d * kvh + f], rt_r.at[slot], blk=tb, uly=my_s * kvh + te)
+            c = remote(src, o.at[slot], rt_s.at[d * kvh + f], rt_r.at[slot], blk=tb, uly=my_s * kvh + te)
             c.start()
             sent.append(c)
     for i in range(heads):
-        arrived(ra.at[i], rt_r.at[i])
-    for h in range(heads):
-        o[:, h * DH : (h + 1) * DH] = ra[slot_of(hm, h, heads, kvh)].reshape(tokens, DH)
+        arrived(o.at[i], rt_r.at[i])
     for c in sent:
         c.wait_send()
+
+
+def place_kernel(kvh, hm, slots, o):
+    heads = hm.shape[0]
+    for h in range(heads):
+        o[:, h * DH : (h + 1) * DH] = slots[slot_of(hm, h, heads, kvh)]
 
 
 def body(queries, keys, values, head_map, doc_lengths, plan):
@@ -231,11 +239,11 @@
     dma = pltpu.SemaphoreType.DMA
     sm = pl.BlockSpec(memory_space=SMEM)
     hbm = pl.BlockSpec(memory_space=pl.ANY)
-    return pl.pallas_call(
+    slots = pl.pallas_call(
         functools.partial(fused_kernel, nb, nz),
-        out_shape=jax.ShapeDtypeStruct((tokens, heads * DH), bf),
-        in_specs=[sm, sm, sm, hbm, hbm, hbm],
-        out_specs=pl.BlockSpec(memory_space=VMEM),
+        out_shape=jax.ShapeDtypeStruct((heads, tokens // block, block, DH), bf),
+        in_specs=[hbm] * 6,
+        out_specs=hbm,
         scratch_shapes=[
             VMEM((tokens, heads * DH), bf),
             VMEM((nb, kvh, tokens, DH), bf),
@@ -246,14 +254,25 @@
             VMEM((2, 2 * nz, nb, part, DH), bf),
             VMEM((pieces, block, DH), bf),
             VMEM((pieces, block, DH), bf),
-            VMEM((heads, tokens // block, block, DH), bf),
             VMEM((tokens, tokens), jnp.float32),
             VMEM((2, tokens, (nz + 1) * tokens), jnp.float32),
-            [dma((n,)) for n in (nb, nb, nb, nb, nz, nz, nz, nz, nz, nz, nb, nb, nb, nb, heads, heads, 2 * kvh + 1)],
+            SMEM(head_map.shape, jnp.int32),
+            SMEM(doc_lengths.shape, jnp.int32),
+            SMEM(plan.shape, jnp.int32),
+            [dma((n,)) for n in (nb, nb, nb, nb, nz, nz, nz, nz, nz, nz, nb, nb, nb, nb, heads, heads, 2 * kvh + 4)],
         ],
         compiler_params=pltpu.CompilerParams(collective_id=0, has_side_effects=True, vmem_limit_bytes=63 << 20),
         name="fused",
     )(head_map, doc_lengths, plan, queries, keys.reshape(nb, part, kvh * DH), values.reshape(nb, part, kvh * DH))
+    vm = pl.BlockSpec(memory_space=VMEM)
+    return pl.pallas_call(
+        functools.partial(place_kernel, kvh),
+        out_shape=jax.ShapeDtypeStruct((tokens, heads * DH), bf),
+        in_specs=[sm, vm],
+        out_specs=vm,
+        compiler_params=pltpu.CompilerParams(vmem_limit_bytes=63 << 20),
+        name="place",
+    )(head_map, slots.reshape(heads, tokens, DH))
 
 
 def solution(mesh):

time: 73.4 us -> 70.7 us (0.963)
  local copies, waits for them, and re-layouts: 1.88 us -> 0 us
  Pallas kernels: 71.3 us -> 70.5 us
    pallas_call x1, Pallas kernels: 71.3 us -> 68.5 us  [body(): pl.pallas_call(functools.partial(fused_kernel, nb, nz), out_shape=jax.Sha...]
    pallas_call x0 -> x1, Pallas kernels: none -> 2.08 us  [body(): pl.pallas_call(functools.partial(place_kernel, kvh), out_shape=jax.ShapeD...]
    unnamed x1 -> x0, local copies, waits for them, and re-layouts: 1.88 us -> none
where the time goes in v4:
time: 70.7 us; the launch traced here: 70.5 us
  Pallas kernels  70.5 us (100%)
    pallas_call x1, Pallas kernels, body(): pl.pallas_call(functools.partial(fused_kernel, nb, nz), out_shape=jax.Sha...  68.5 us
    pallas_call x1, Pallas kernels, body(): pl.pallas_call(functools.partial(place_kernel, kvh), out_shape=jax.ShapeD...  2.08 us

profile of v4, /device:TPU:1, one launch (start us, length us, event | category | flops | bytes accessed | tf_op | source)
XLA Modules:
  0.0 70.5 jit_solution(12474952800233585133)
XLA Ops:
  0.0 68.5 %fused.1 = bf16[16,2,64,128]{3,2,1,0:T(8,128)(2,1)} custom-call(s32[16]{0:T(128)} %hm.1, s32[32]{0:T(128)} %lengths_hbm.1, s32[8,32]{1,0:T(8,128)} %plan_hbm.1, bf16[128,2048]{1,0:T(8,128)(2,1)} %q_hbm.1, bf16[8,16,256]{2,1,0:T(8,128)(2,1)} %bitcast.4, bf16[8,16,256]{2,1,0:T(8,128)(2,1)} %bitcast.5), custom_call_target="tpu_custom_call" | custom-call | tf_op jit(solution)/shard_map/fused/pallas_call | solution.py:242
  68.5 2.1 %place.1 = bf16[128,2048]{1,0:T(8,128)(2,1)} custom-call(s32[16]{0:T(128)} %hm.1, bf16[16,128,128]{2,1,0:T(8,128)(2,1)} %bitcast.3), custom_call_target="tpu_custom_call" | custom-call | tf_op jit(solution)/shard_map/place/pallas_call | solution.py:268

commit v5 on v4

--- a/solution.py
+++ b/solution.py
@@ -45,10 +45,10 @@
 
     barrier = pltpu.get_barrier_semaphore()
     twin = [(d, f) for f in range(1, kvh) for d in range(1, nb)]
+    for d in sorted(range(1, nz), key=lambda d: -min(d, nz - d)):
+        pl.semaphore_signal(barrier, inc=1, device_id={"uly": lax.rem(u + d, nz)}, device_id_type=MESH)
     for d in range(1, nb):
         pl.semaphore_signal(barrier, inc=1, device_id={"blk": lax.rem(b + d, nb)}, device_id_type=MESH)
-    for d in range(1, nz):
-        pl.semaphore_signal(barrier, inc=1, device_id={"uly": lax.rem(u + d, nz)}, device_id_type=MESH)
     for d, f in twin:
         pl.semaphore_signal(
             barrier, inc=1, device_id={"blk": lax.rem(b + d, nb), "uly": my_s * kvh + lax.rem(my_e + f, kvh)},
@@ -202,12 +202,13 @@
 
     lax.fori_loop(0, nz // 2, two_tiles, 0)
 
-    for i in range(pieces):
-        sa[i] = att[plan[my_s, i]]
     slot = my_e * nb + b
     for d, f in [(d, f) for f in range(kvh - 1, -1, -1) for d in near[::-1]] + [(0, f) for f in range(kvh - 1, -1, -1)]:
         tb, te = lax.rem(b + d, nb), lax.rem(my_e + f, kvh)
-        src = sa.at[pl.ds((tb * kvh + te) * per, per)]
+        at = (tb * kvh + te) * per
+        for i in range(per):
+            sa[at + i] = att[plan[my_s, at + i]]
+        src = sa.at[pl.ds(at, per)]
         if (d, f) == (0, 0):
             pltpu.make_async_copy(src, o.at[slot], rt_r.at[slot]).start()
         else:
@@ -220,10 +221,27 @@
         c.wait_send()
 
 
-def place_kernel(kvh, hm, slots, o):
-    heads = hm.shape[0]
-    for h in range(heads):
-        o[:, h * DH : (h + 1) * DH] = slots[slot_of(hm, h, heads, kvh)]
+def place_kernel(kvh, parts, hm_hbm, slots, o, hm, x, y, in_s, out_s, hm_s):
+    heads, tokens = x.shape[0], x.shape[1]
+    rows = tokens // parts
+    get_hm = pltpu.make_async_copy(hm_hbm, hm, hm_s.at[0])
+    get_hm.start()
+    gets, puts = [], []
+    for t in range(parts):
+        at = slice(t * rows, (t + 1) * rows)
+        gets.append(pltpu.make_async_copy(slots.at[:, at], x.at[:, at], in_s.at[t]))
+        puts.append(pltpu.make_async_copy(y.at[at], o.at[at], out_s.at[t]))
+        gets[t].start()
+    get_hm.wait()
+    source = [slot_of(hm, h, heads, kvh) for h in range(heads)]
+    for t in range(parts):
+        at = slice(t * rows, (t + 1) * rows)
+        gets[t].wait()
+        for h in range(heads):
+            y[at, h * DH : (h + 1) * DH] = x[source[h], at]
+        puts[t].start()
+    for c in puts:
+        c.wait()
 
 
 def body(queries, keys, values, head_map, doc_lengths, plan):
@@ -237,7 +255,6 @@
     block = stretch // pieces
     bf = jnp.bfloat16
     dma = pltpu.SemaphoreType.DMA
-    sm = pl.BlockSpec(memory_space=SMEM)
     hbm = pl.BlockSpec(memory_space=pl.ANY)
     slots = pl.pallas_call(
         functools.partial(fused_kernel, nb, nz),
@@ -264,12 +281,20 @@
         compiler_params=pltpu.CompilerParams(collective_id=0, has_side_effects=True, vmem_limit_bytes=63 << 20),
         name="fused",
     )(head_map, doc_lengths, plan, queries, keys.reshape(nb, part, kvh * DH), values.reshape(nb, part, kvh * DH))
-    vm = pl.BlockSpec(memory_space=VMEM)
+    parts = 4
     return pl.pallas_call(
-        functools.partial(place_kernel, kvh),
+        functools.partial(place_kernel, kvh, parts),
         out_shape=jax.ShapeDtypeStruct((tokens, heads * DH), bf),
-        in_specs=[sm, vm],
-        out_specs=vm,
+        in_specs=[hbm, hbm],
+        out_specs=hbm,
+        scratch_shapes=[
+            SMEM(head_map.shape, jnp.int32),
+            VMEM((heads, tokens, DH), bf),
+            VMEM((tokens, heads * DH), bf),
+            dma((parts,)),
+            dma((parts,)),
+            dma((1,)),
+        ],
         compiler_params=pltpu.CompilerParams(vmem_limit_bytes=63 << 20),
         name="place",
     )(head_map, slots.reshape(heads, tokens, DH))

time: 70.7 us -> 70.3 us (level)
  no operation moved by 1% of the time
where the time goes in v5:
time: 70.3 us; the launch traced here: 70.1 us
  Pallas kernels  70.1 us (100%)
    pallas_call x1, Pallas kernels, body(): pl.pallas_call(functools.partial(fused_kernel, nb, nz), out_shape=jax.Sha...  68.2 us
    pallas_call x1, Pallas kernels, body(): pl.pallas_call(functools.partial(place_kernel, kvh, parts), out_shape=jax...  1.87 us

profile of v5, /device:TPU:1, one launch (start us, length us, event | category | flops | bytes accessed | tf_op | source)
XLA Modules:
  0.0 70.1 jit_solution(272585183395212161)
XLA Ops:
  0.0 68.2 %fused.1 = bf16[16,2,64,128]{3,2,1,0:T(8,128)(2,1)} custom-call(s32[16]{0:T(128)} %hm_hbm.3, s32[32]{0:T(128)} %lengths_hbm.1, s32[8,32]{1,0:T(8,128)} %plan_hbm.1, bf16[128,2048]{1,0:T(8,128)(2,1)} %q_hbm.1, bf16[8,16,256]{2,1,0:T(8,128)(2,1)} %bitcast.4, bf16[8,16,256]{2,1,0:T(8,128)(2,1)} %bitcast.5), custom_call_target="tpu_custom_call" | custom-call | tf_op jit(solution)/shard_map/fused/pallas_call | solution.py:259
  68.2 1.9 %place.1 = bf16[128,2048]{1,0:T(8,128)(2,1)} custom-call(s32[16]{0:T(128)} %hm_hbm.3, bf16[16,128,128]{2,1,0:T(8,128)(2,1)} %bitcast.3), custom_call_target="tpu_custom_call" | custom-call | tf_op jit(solution)/shard_map/place/pallas_call | solution.py:285

commit v6 on v5

--- a/solution.py
+++ b/solution.py
@@ -143,7 +143,7 @@
         for z in range(nz):
             arrived(kvo.at[:, cp * nz + z, b], rs.at[z])
         mine = kvo.at[:, cp * nz : (cp + 1) * nz, b]
-        for d in range(1, half):
+        for d in sorted(range(1, half), key=lambda d: -min(d, half - d)):
             c = remote(mine, mine, gy_s.at[cp * half + d], gy_r.at[cp * half + d], blk=lax.rem(b + 2 * d, nb))
             c.start()
             sent.append(c)
@@ -151,7 +151,7 @@
         c.start()
         sent.append(c)
     for cp in (1, 0):
-        for d in range(1, half):
+        for d in sorted(range(1, half), key=lambda d: min(d, half - d)):
             block = kvo.at[:, cp * nz : (cp + 1) * nz, lax.rem(b + nb - 2 * d, nb)]
             arrived(block, gy_r.at[cp * half + d])
             c = remote(block, block, gc_s.at[cp * half + d], gc_r.at[cp * half + d], blk=other)

time: 70.3 us -> 70.3 us (level)
  no operation moved by 1% of the time
where the time goes in v6:
time: 70.3 us; the launch traced here: 70.1 us
  Pallas kernels  70.1 us (100%)
    pallas_call x1, Pallas kernels, body(): pl.pallas_call(functools.partial(fused_kernel, nb, nz), out_shape=jax.Sha...  68.2 us
    pallas_call x1, Pallas kernels, body(): pl.pallas_call(functools.partial(place_kernel, kvh, parts), out_shape=jax...  1.87 us

profile of v6, /device:TPU:1, one launch (start us, length us, event | category | flops | bytes accessed | tf_op | source)
XLA Modules:
  0.0 70.1 jit_solution(4982943862052166043)
XLA Ops:
  0.0 68.2 %fused.1 = bf16[16,2,64,128]{3,2,1,0:T(8,128)(2,1)} custom-call(s32[16]{0:T(128)} %hm_hbm.3, s32[32]{0:T(128)} %lengths_hbm.1, s32[8,32]{1,0:T(8,128)} %plan_hbm.1, bf16[128,2048]{1,0:T(8,128)(2,1)} %q_hbm.1, bf16[8,16,256]{2,1,0:T(8,128)(2,1)} %bitcast.4, bf16[8,16,256]{2,1,0:T(8,128)(2,1)} %bitcast.5), custom_call_target="tpu_custom_call" | custom-call | tf_op jit(solution)/shard_map/fused/pallas_call | solution.py:259
  68.2 1.9 %place.1 = bf16[128,2048]{1,0:T(8,128)(2,1)} custom-call(s32[16]{0:T(128)} %hm_hbm.3, bf16[16,128,128]{2,1,0:T(8,128)(2,1)} %bitcast.3), custom_call_target="tpu_custom_call" | custom-call | tf_op jit(solution)/shard_map/place/pallas_call | solution.py:285
